TPU v7x, 256 devices: a whole 4x4x8 slice. The times are simulated.
256 devices in a mesh: row: 16 (over x_hi, z), col: 16 (over y, x_lo, core).
Axes of the slice: x: 4 (x_hi: 2, x_lo: 2; x = x_hi * 2 + x_lo), y: 4, z: 8, core: 2. Of those that a mesh axis runs over, the one named last changes fastest.
Arguments:
- start_block: bfloat16 [256, 16384], P('row', 'col'), may hold values from -6 to 6
- stiffness: bfloat16 [16, 16, 64, 128, 128], P('row', 'col'), as said below
- mass: bfloat16 [16, 16, 64, 128, 128], P('row', 'col'), as said below
- block_coords: int32 [16, 16, 64, 2], P('row', 'col'), may hold values from -1 to 7, as said below
- lower_bound: float32 [1], replicated, may hold values from 0 to 0.4
- upper_bound: float32 [1], replicated, may hold values from 1.6 to 2.4
Outputs:
- filtered: float32 [256, 16384], P('col', 'row')
Inputs may be any that keep to these rules, and one draw needn't show every extreme that they name: `block_coords`: slot s of tile (r, c) names a block row and block column within the tile, or (-1, -1) when it is empty; live slots come before empty ones and no block is named twice. The pattern is symmetric: block (I, J) is live exactly when block (J, I) is, and every diagonal block is live. `stiffness`: K is symmetric: the slot of block (J, I) holds the transpose of the slot of block (I, J), and diagonal blocks are symmetric. `mass`: M is symmetric in the same way as K, on the same pattern.
All inputs are finite; a program needn't handle non-finite values.
Results may differ from a plain program's by a relative error of at most 0.0033.
Values may be sent and summed in bfloat16 or wider, within the bound.
A program may use at most 64 MiB of HBM per device.

v0:
```python
import jax
import jax.numpy as jnp
from jax import lax
from jax.sharding import PartitionSpec as P

BLK = 128
BR = 8


def local_terms(vecs, kvals, mvals, source_idx, target_idx, ntarget, centre, scale, forward):
    width = vecs.shape[0]
    nsource = vecs.shape[1] // BLK
    blocks = vecs.reshape(width, nsource, BLK)
    picked = jnp.take(blocks, jnp.clip(source_idx, 0, nsource - 1), axis=1)
    if forward:
        kpart = jnp.einsum("psj,sij->psi", picked, kvals, preferred_element_type=jnp.float32)
        mpart = jnp.einsum("psj,sij->psi", picked, mvals, preferred_element_type=jnp.float32)
    else:
        kpart = jnp.einsum("psi,sij->psj", picked, kvals, preferred_element_type=jnp.float32)
        mpart = jnp.einsum("psi,sij->psj", picked, mvals, preferred_element_type=jnp.float32)
    terms = (kpart - centre * mpart) * scale
    placing = (target_idx[:, None] == jnp.arange(ntarget, dtype=jnp.int32)[None, :]).astype(
        jnp.float32
    )
    placed = jnp.einsum("psi,sb->pbi", terms, placing, precision=lax.Precision.HIGHEST)
    return placed.reshape(width, ntarget * BLK)


def local(start_block, stiffness, mass, block_coords, lower_bound, upper_bound):
    kvals = stiffness[0, 0]
    mvals = mass[0, 0]
    coords = block_coords[0, 0]
    tile_rows = coords[:, 0]
    tile_cols = coords[:, 1]
    ncols = start_block.shape[1] // BLK
    centre = 0.5 * (lower_bound[0] + upper_bound[0])
    half = 0.5 * (upper_bound[0] - lower_bound[0])
    first_scale = 1.0 / half
    next_scale = 2.0 / half

    def forward_terms(source, scale):
        return local_terms(source, kvals, mvals, tile_cols, tile_rows, BR, centre, scale, True)

    vectors = lax.all_gather(start_block, "row", axis=0, tiled=True)
    first = lax.psum_scatter(
        forward_terms(vectors, first_scale), "col", scatter_dimension=0, tiled=True
    ).astype(jnp.bfloat16)
    spread = lax.all_gather(first, "col", axis=0, tiled=True)
    second_sum = lax.psum_scatter(
        local_terms(spread, kvals, mvals, tile_rows, tile_cols, ncols, centre, next_scale, False),
        "row",
        scatter_dimension=0,
        tiled=True,
    )
    second = (second_sum - start_block.astype(jnp.float32)).astype(jnp.bfloat16)
    widened = lax.all_gather(second, "row", axis=0, tiled=True)
    third_sum = lax.psum_scatter(
        forward_terms(widened, next_scale), "col", scatter_dimension=0, tiled=True
    )
    filtered = third_sum - first.astype(jnp.float32)
    return filtered


def solution(mesh):
    placed = (
        P("row", "col"),
        P("row", "col", None, None, None),
        P("row", "col", None, None, None),
        P("row", "col", None, None),
        P(),
        P(),
    )
    return jax.shard_map(
        local, mesh=mesh, in_specs=placed, out_specs=P("col", "row"), check_vma=False
    )
```

profile of v0, /device:TPU:4, one launch (start us, length us, event | category | flops | bytes accessed | tf_op | source)
XLA Modules:
  0.0 517.8 jit_solution(6235305104215653185)
XLA Ops:
  8.0 0.8 slice_bitcast_fusion
  8.7 0.8 compare_and_fusion.1
  9.5 44.7 %all_gather.9 = bf16[256,1024]{1,0:T(8,128)(2,1)S(1)} all-gather(bf16[16,1024]{1,0:T(8,128)(2,1)} %param.8), channel_id=1, replica_groups=mesh['row'=16,'col'=16] {'row'}, dimensions={0}, use_global_device_ids=true | all-gather | bytes 557056 | tf_op jit(solution)/shard_map/all_gather | solution.py:44
  54.4 0.3 copy.36
  54.8 3.0 gather_fusion
  57.8 6.9 %fusion.14 = f32[64,256,128]{2,1,0:T(8,128)} fusion(bf16[1,1,64,128,128]{4,3,2,1,0:T(8,128)(2,1)S(1)} %copy-done, bf16[64,256,128]{2,1,0:T(8,128)(2,1)} %gather_fusion, pred[64]{0:T(512)(128)(4,1)S(1)} %get-tuple-element.12), kind=kOutput, calls=%fused_computation.20 | convolution fusion | flops 538968064 | bytes 14680128 | tf_op jit(solution)/shard_map/psj,sij->psi/dot_general | solution.py:17
  64.7 4.8 multiply_bitcast_fusion.2
  69.5 7.5 %fusion.30 = f32[256,8,128]{2,1,0:T(8,128)S(1)} fusion(f32[256,64,128]{2,0,1:T(8,128)S(1)} %multiply_bitcast_fusion.2, s32[64]{0:T(128)S(1)} %get-tuple-element.11), kind=kOutput, calls=%fused_computation.33 | convolution fusion | flops 201327104 | bytes 9437440 | tf_op jit(solution)/shard_map/psi,sb->pbi/dot_general | solution.py:25
  77.0 1.4 copy.50
  78.4 2.7 copy.53
  81.2 60.7 %reduce-scatter.10.cloned.1.call-done = f32[16,1024]{1,0:T(8,128)} async-done(((f32[256,1024]{1,0:T(8,128)}), f32[16,1024]{1,0:T(8,128)}) %reduce-scatter.10.cloned.1.call-update) | async-done | bytes 65552 | tf_op jit(solution)/shard_map/reduce_scatter | solution.py:45
  141.9 0.8 convert_element_type.15
  142.7 19.0 %all_gather.10 = bf16[256,1024]{1,0:T(8,128)(2,1)S(1)} all-gather(bf16[16,1024]{1,0:T(8,128)(2,1)S(1)} %convert_element_type.15), channel_id=1, replica_groups=mesh['row'=16,'col'=16] {'col'}, dimensions={0}, use_global_device_ids=true | all-gather | bytes 557056 | tf_op jit(solution)/shard_map/all_gather | solution.py:48
  161.9 0.3 copy.41
  162.2 3.0 gather_fusion.1
  165.3 3.6 fusion.10
  168.9 3.0 multiply_bitcast_fusion.1
  171.9 7.5 %fusion.33 = f32[256,8,128]{2,1,0:T(8,128)S(1)} fusion(f32[256,64,128]{2,0,1:T(8,128)S(1)} %multiply_bitcast_fusion.1, s32[64]{0:T(128)S(1)} %get-tuple-element.10), kind=kOutput, calls=%fused_computation.34 | convolution fusion | flops 201327104 | bytes 9437440 | tf_op jit(solution)/shard_map/psi,sb->pbi/dot_general | solution.py:25
  179.4 1.4 copy.51
  180.8 2.7 copy.55
  183.6 196.9 %reduce-scatter.12.cloned.1.call-done = f32[16,1024]{1,0:T(8,128)} async-done(((f32[256,1024]{1,0:T(8,128)}), f32[16,1024]{1,0:T(8,128)}) %reduce-scatter.12.cloned.1.call-update) | async-done | bytes 65552 | tf_op jit(solution)/shard_map/reduce_scatter | solution.py:49
  380.5 0.8 subtract_convert_fusion
  381.3 41.5 %all_gather.11 = bf16[256,1024]{1,0:T(8,128)(2,1)S(1)} all-gather(bf16[16,1024]{1,0:T(8,128)(2,1)S(1)} %subtract_convert_fusion), channel_id=1, replica_groups=mesh['row'=16,'col'=16] {'row'}, dimensions={0}, use_global_device_ids=true | all-gather | bytes 557056 | tf_op jit(solution)/shard_map/all_gather | solution.py:56
  423.0 0.3 copy.46
  423.3 3.0 gather_fusion.2
  426.3 6.9 %fusion.6 = f32[64,256,128]{2,1,0:T(8,128)} fusion(bf16[1,1,64,128,128]{4,3,2,1,0:T(8,128)(2,1)S(1)} %copy-done, bf16[64,256,128]{2,1,0:T(8,128)(2,1)} %gather_fusion.2, pred[64]{0:T(512)(128)(4,1)S(1)} %get-tuple-element.12), kind=kOutput, calls=%fused_computation.12 | convolution fusion | flops 538968064 | bytes 14680128 | tf_op jit(solution)/shard_map/psj,sij->psi/dot_general | solution.py:17
  433.2 4.8 multiply_bitcast_fusion
  438.0 7.5 %fusion.36 = f32[256,8,128]{2,1,0:T(8,128)S(1)} fusion(f32[256,64,128]{2,0,1:T(8,128)S(1)} %multiply_bitcast_fusion, s32[64]{0:T(128)S(1)} %get-tuple-element.11), kind=kOutput, calls=%fused_computation.35 | convolution fusion | flops 201327104 | bytes 9437440 | tf_op jit(solution)/shard_map/psi,sb->pbi/dot_general | solution.py:25
  445.5 1.4 copy.52
  446.9 2.5 copy.57
  449.5 60.0 %reduce-scatter.14.cloned.1.call-done = f32[16,1024]{1,0:T(8,128)} async-done(((f32[256,1024]{1,0:T(8,128)}), f32[16,1024]{1,0:T(8,128)}) %reduce-scatter.14.cloned.1.call-update) | async-done | bytes 65552 | tf_op jit(solution)/shard_map/reduce_scatter | solution.py:57
  509.5 1.5 convert_subtract_fusion
  (26 shorter events, 0.8 us)
Async XLA Ops:
  6.5 51.3 %copy-start = (bf16[1,1,64,128,128]{4,3,2,1,0:T(8,128)(2,1)S(1)}, bf16[1,1,64,128,128]{4,3,2,1,0:T(8,128)(2,1)}, u32[]{:S(2)}) copy-start(bf16[1,1,64,128,128]{4,3,2,1,0:T(8,128)(2,1)} %param.10) | copy-start | bytes 6291460
  6.5 135.3 %reduce-scatter.10.cloned.1.call-start = ((), (), s32[]{:S(2)}) async-start(), calls=%async_computation.3 | async-start | bytes 1114112 | tf_op jit(solution)/shard_map/reduce_scatter | solution.py:45
  57.8 6.9 %copy-start.3 = (bf16[64,256,128]{2,1,0:T(8,128)(2,1)S(1)}, bf16[64,256,128]{2,1,0:T(8,128)(2,1)}, u32[]{:S(2)}) copy-start(bf16[64,256,128]{2,1,0:T(8,128)(2,1)} %gather_fusion) | copy-start | bytes 12582916
  57.8 6.9 %copy-start.4 = (bf16[1,1,64,128,128]{4,3,2,1,0:T(8,128)(2,1)S(1)}, bf16[1,1,64,128,128]{4,3,2,1,0:T(8,128)(2,1)}, u32[]{:S(2)}) copy-start(bf16[1,1,64,128,128]{4,3,2,1,0:T(8,128)(2,1)} %param.9) | copy-start | bytes 6291460
  81.1 299.3 %reduce-scatter.12.cloned.1.call-start = ((), (), s32[]{:S(2)}) async-start(), calls=%async_computation.4 | async-start | bytes 1114112 | tf_op jit(solution)/shard_map/reduce_scatter | solution.py:49
  165.3 3.6 copy-start.2
  179.4 201.1 %copy-start.7 = (bf16[16,1024]{1,0:T(8,128)(2,1)S(1)}, bf16[16,1024]{1,0:T(8,128)(2,1)}, u32[]{:S(2)}) copy-start(bf16[16,1024]{1,0:T(8,128)(2,1)} %param.8) | copy-start | bytes 98308
  183.5 325.9 %reduce-scatter.14.cloned.1.call-start = ((), (), s32[]{:S(2)}) async-start(), calls=%async_computation.5 | async-start | bytes 1114112 | tf_op jit(solution)/shard_map/reduce_scatter | solution.py:57
  426.3 6.9 %copy-start.1 = (bf16[64,256,128]{2,1,0:T(8,128)(2,1)S(1)}, bf16[64,256,128]{2,1,0:T(8,128)(2,1)}, u32[]{:S(2)}) copy-start(bf16[64,256,128]{2,1,0:T(8,128)(2,1)} %gather_fusion.2) | copy-start | bytes 12582916
  426.3 6.9 %copy-start.5 = (bf16[1,1,64,128,128]{4,3,2,1,0:T(8,128)(2,1)S(1)}, bf16[1,1,64,128,128]{4,3,2,1,0:T(8,128)(2,1)}, u32[]{:S(2)}) copy-start(bf16[1,1,64,128,128]{4,3,2,1,0:T(8,128)(2,1)} %param.9) | copy-start | bytes 6291460
  445.5 64.0 %copy-start.6 = (f32[16,1024]{1,0:T(8,128)S(1)}, f32[16,1024]{1,0:T(8,128)}, u32[]{:S(2)}) copy-start(f32[16,1024]{1,0:T(8,128)} %reduce-scatter.10.cloned.1.call-done) | copy-start | bytes 196612
Sparse Core Ops, SparseCore 0:
  81.2 60.5 reduce-scatter.9
  183.6 196.7 reduce-scatter.11
  449.6 59.8 reduce-scatter.13
where the time goes:
time: 527 us; the launch traced here: 518 us
  waiting for transfers between devices  318 us (60%)
  blocking collectives  105 us (20%)
  matrix products  52.4 us (10%)
  local copies, waits for them, and re-layouts  23.5 us (4%)
  between operations  15.1 us (3%)
    reduce_scatter x1, waiting for transfers between devices, local(): lax.psum_scatter(local_terms(spread, kvals, mvals, tile_rows, tile_cols,...  197 us
    reduce_scatter x1, waiting for transfers between devices, local(): lax.psum_scatter(forward_terms(vectors, first_scale), 'col', scatter_dime...  60.7 us
    reduce_scatter x1, waiting for transfers between devices, local(): lax.psum_scatter(forward_terms(widened, next_scale), 'col', scatter_dimen...  60 us
    all_gather x1, blocking collectives, local(): vectors = lax.all_gather(start_block, 'row', axis=0, tiled=True)  44.7 us
    all_gather x1, blocking collectives, local(): widened = lax.all_gather(second, 'row', axis=0, tiled=True)  41.5 us
    dot_general x3, matrix products, local_terms(): jnp.einsum('psi,sb->pbi', terms, placing, precision=lax.Precision.HIGHEST)  22.5 us
    all_gather x1, blocking collectives, local(): spread = lax.all_gather(first, 'col', axis=0, tiled=True)  19 us
    dot_general x2, matrix products, local_terms(): jnp.einsum('psj,sij->psi', picked, mvals, preferred_element_type=jnp.floa...  13.7 us
  transfers between devices with their start and end apart: 3, of which 3 were waited for; matrix products, arithmetic and copies ran while one was open for 0% of the time, Pallas kernels for 0%

commit v1 on v0

v1 whole, which is shorter than its diff:
```python
import jax
import jax.numpy as jnp
from jax import lax
from jax.experimental import pallas as pl
from jax.experimental.pallas import tpu as pltpu
from jax.sharding import PartitionSpec as P

MESH = pl.DeviceIdType.MESH
BLK = 128
BR = 8
TILE = 1024
PIECE = 16
NS = 8
TOP = 32766.0
TINY = 1e-33
ROW_NEAR = (1, 7, 2, 6, 3, 5, 4)
ROW_FAR = (4, 3, 5, 2, 6, 1, 7)
COL_NEAR = (4, 1, 3, 5, 7, 2, 6)
COL_FAR = (6, 2, 5, 7, 1, 3, 4)


def back(axis, o):
    return (-o) % NS if axis == "row" else (o // 4) * 4 + (-o) % 4


def rem(a, b):
    return lax.rem(a, jnp.int32(b))


def div(a, b):
    return lax.div(a, jnp.int32(b))


def flip(bit, s):
    return 1 - bit if s else bit


def kernel(inv, lower, upper, start, khbm, mhbm, out, kslot, mslot, kd, md, ybuf, ag, qsib, rsib, qring, rring, own, keep,
           s_sib, s_ring, r_sib, r_ring, local_sem, send_sem, recv_sem, ssend_sem, srecv_sem):
    r = lax.axis_index("row")
    c = lax.axis_index("col")
    xh, z = div(r, NS), rem(r, NS)
    y, xl, core = div(c, 4), rem(div(c, 2), 2), rem(c, 2)

    def member(axis, s, o):
        if axis == "row":
            return flip(xh, s) * NS + rem(z + o, NS)
        return rem(y + o % 4, 4) * 4 + flip(xl, o // 4) * 2 + flip(core, s)

    def device(axis, s, o):
        m = member(axis, s, o)
        return (m, c) if axis == "row" else (r, m)

    kcopy = pltpu.make_async_copy(khbm, kslot, local_sem.at[0])
    mcopy = pltpu.make_async_copy(mhbm, mslot, local_sem.at[1])
    kcopy.start()
    mcopy.start()

    barrier = pltpu.get_barrier_semaphore()
    for axis in ("row", "col"):
        for o in range(1, NS):
            pl.semaphore_signal(barrier, inc=1, device_id=device(axis, 0, o), device_id_type=MESH)
        pl.semaphore_signal(barrier, inc=1, device_id=device(axis, 1, 0), device_id_type=MESH)

    centre = 0.5 * (lower[0] + upper[0])
    half = 0.5 * (upper[0] - lower[0])

    kcopy.wait()
    mcopy.wait()
    for t in range(BR * BR):
        s = inv[t]
        live = s >= 0
        s = jnp.maximum(s, 0)
        rows, cols = pl.ds((t // BR) * BLK, BLK), pl.ds((t % BR) * BLK, BLK)
        kd[rows, cols] = jnp.where(live, kslot[s], jnp.zeros((BLK, BLK), jnp.bfloat16))
        md[rows, cols] = jnp.where(live, mslot[s], jnp.zeros((BLK, BLK), jnp.bfloat16))

    pl.semaphore_wait(barrier, 2 * NS)

    sent = []

    def copy(n, side, src, dst, i, j, dev, sems=(send_sem, recv_sem)):
        return pltpu.make_async_remote_copy(
            src_ref=src, dst_ref=dst, send_sem=sems[0].at[n, side, i], recv_sem=sems[1].at[n, side, j],
            device_id=dev, device_id_type=MESH)

    def push(*args, **kw):
        one = copy(*args, **kw)
        one.start()
        sent.append(one)

    def arrived(n, side, dst, j, sems=(send_sem, recv_sem)):
        copy(n, side, dst, dst, 0, j, (r, c), sems).wait_recv()

    def gather(g, n, axis, src, order_out, order_in):
        buf = ag.at[g]
        push(n, 1, src, buf.at[NS], 0, 0, device(axis, 1, 0))
        for o in order_out:
            j = back(axis, o)
            push(n, 0, src, buf.at[j], o, j, device(axis, 0, o))
        buf[0] = src[...]
        for o in order_in:
            arrived(n, 0, buf.at[o], o)
            push(n, 1, buf.at[o], buf.at[NS + o], o, o, device(axis, 1, 0))
        for o in (0,) + order_in:
            arrived(n, 1, buf.at[NS + o], o)

    def quantize(part, q, sc):
        top = jnp.maximum(jnp.max(jnp.abs(part), keepdims=True), TINY)
        q[...] = jnp.round(part * (TOP / top)).astype(jnp.int32).astype(jnp.int16)
        sc[...] = jnp.broadcast_to(top * (1.0 / TOP), (1, BLK))

    def value(q, sc):
        return q[...].astype(jnp.int32).astype(jnp.float32) * sc[:, :1]

    scale_sems = (ssend_sem, srecv_sem)

    def scatter(m, n, axis, order):
        for o in order + (0,):
            quantize(ybuf[NS + o], qsib.at[m, o], s_sib.at[m, o])
            push(n, 1, qsib.at[m, o], rsib.at[m, o], o, o, device(axis, 1, 0))
            push(n, 1, s_sib.at[m, o], r_sib.at[m, o], o, o, device(axis, 1, 0), scale_sems)
        total = None
        for o in order + (0,):
            arrived(n, 1, rsib.at[m, o], o)
            arrived(n, 1, r_sib.at[m, o], o, scale_sems)
            part = ybuf[o] + value(rsib.at[m, o], r_sib.at[m, o])
            if o:
                j = back(axis, o)
                quantize(part, qring.at[m, o], s_ring.at[m, o])
                push(n, 0, qring.at[m, o], rring.at[m, j], o, j, device(axis, 0, o))
                push(n, 0, s_ring.at[m, o], r_ring.at[m, j], o, j, device(axis, 0, o), scale_sems)
            else:
                total = part
        own[...] = total
        for o in reversed(order):
            arrived(n, 0, rring.at[m, o], o)
            arrived(n, 0, r_ring.at[m, o], o, scale_sems)
            own[...] += value(rring.at[m, o], r_ring.at[m, o])
        return own[...]

    def product(g, come, go, scale, transposed):
        rows = []
        for s in (0, 1):
            for o in range(NS):
                v = member(go, s, o)
                if come == "row":
                    slot = rem(div(v, NS) + xh, 2) * NS + rem(rem(v, NS) - z + NS, NS)
                else:
                    slot = rem(v + core, 2) * NS + rem(div(v, 2) + xl, 2) * 4 + rem(div(v, 4) - y + 4, 4)
                rows.append(ag[g, slot])
        x = jnp.concatenate(rows, axis=0)
        dims = (((1,), (1,)), ((), ())) if transposed else (((1,), (0,)), ((), ()))
        kpart = lax.dot_general(x, kd[...], dims, preferred_element_type=jnp.float32)
        mpart = lax.dot_general(x, md[...], dims, preferred_element_type=jnp.float32)
        ybuf[...] = ((kpart - centre * mpart) * scale).reshape(2 * NS, PIECE, TILE)

    gather(0, 0, "row", start, ROW_NEAR, ROW_NEAR)
    product(0, "row", "col", 1.0 / half, True)
    keep[0] = scatter(0, 1, "col", COL_FAR).astype(jnp.bfloat16)
    gather(1, 2, "col", keep.at[0], COL_FAR, COL_NEAR)
    product(1, "col", "row", 2.0 / half, False)
    keep[1] = (scatter(1, 3, "row", ROW_FAR) - start[...].astype(jnp.float32)).astype(jnp.bfloat16)
    gather(2, 4, "row", keep.at[1], ROW_NEAR, ROW_NEAR)
    product(2, "row", "col", 2.0 / half, True)
    out[...] = scatter(2, 5, "col", COL_FAR) - keep[0].astype(jnp.float32)
    for one in sent:
        one.wait_send()


def local(start, stiffness, mass, coords, lower, upper):
    pairs = coords[0, 0]
    place = jnp.where(pairs[:, 0] < 0, -1, pairs[:, 0] * BR + pairs[:, 1])
    slots = place.shape[0]
    found = place[None, :] == jnp.arange(BR * BR, dtype=jnp.int32)[:, None]
    inv = jnp.max(jnp.where(found, jnp.arange(slots, dtype=jnp.int32)[None, :], -1), axis=1)
    smem, vmem, hbm = (pl.BlockSpec(memory_space=m) for m in (pltpu.SMEM, pltpu.VMEM, pl.ANY))
    half = (3, NS, PIECE, TILE)
    scales = pltpu.VMEM((3, NS, 1, BLK), jnp.float32)
    sems = pltpu.SemaphoreType.DMA((6, 2, NS))
    return pl.pallas_call(
        kernel,
        out_shape=jax.ShapeDtypeStruct(start.shape, jnp.float32),
        in_specs=[smem, smem, smem, vmem, hbm, hbm],
        out_specs=vmem,
        scratch_shapes=[
            pltpu.VMEM((slots, BLK, BLK), jnp.bfloat16),
            pltpu.VMEM((slots, BLK, BLK), jnp.bfloat16),
            pltpu.VMEM((TILE, TILE), jnp.bfloat16),
            pltpu.VMEM((TILE, TILE), jnp.bfloat16),
            pltpu.VMEM((2 * NS, PIECE, TILE), jnp.float32),
            pltpu.VMEM((3, 2 * NS, PIECE, TILE), jnp.bfloat16),
            pltpu.VMEM(half, jnp.int16),
            pltpu.VMEM(half, jnp.int16),
            pltpu.VMEM(half, jnp.int16),
            pltpu.VMEM(half, jnp.int16),
            pltpu.VMEM((PIECE, TILE), jnp.float32),
            pltpu.VMEM((2, PIECE, TILE), jnp.bfloat16),
            scales, scales, scales, scales,
            pltpu.SemaphoreType.DMA((2,)),
            sems, sems, sems, sems,
        ],
        compiler_params=pltpu.CompilerParams(
            collective_id=0, has_side_effects=True, vmem_limit_bytes=56 * 2**20
        ),
        name="filter",
    )(inv, lower, upper, start, stiffness.reshape(stiffness.shape[2:]), mass.reshape(mass.shape[2:]))


def solution(mesh):
    placed = (
        P("row", "col"),
        P("row", "col", None, None, None),
        P("row", "col", None, None, None),
        P("row", "col", None, None),
        P(),
        P(),
    )
    return jax.shard_map(
        local, mesh=mesh, in_specs=placed, out_specs=P("col", "row"), check_vma=False
    )
```

time: 527 us -> 82.5 us (0.16)
  the two profiles are of different devices: /device:TPU:4 before, /device:TPU:1 now
where the time goes in v1:
time: 82.5 us; the launch traced here: 82.2 us
  Pallas kernels  78.1 us (95%)
  local copies, waits for them, and re-layouts  1.47 us (2%)
  other arithmetic  1.39 us (2%)
  between operations  1.31 us (2%)
    pallas_call x1, Pallas kernels, local(): pl.pallas_call(kernel, out_shape=jax.ShapeDtypeStruct(start.shape, jnp.fl...  78.1 us

profile of v1, /device:TPU:1, one launch (start us, length us, event | category | flops | bytes accessed | tf_op | source)
XLA Modules:
  0.0 82.2 jit_solution(6193379026534786053)
XLA Ops:
  1.3 0.8 fusion
  2.1 0.6 select_reduce_fusion.inv
  2.7 78.1 %filter.1 = f32[16,1024]{1,0:T(8,128)} custom-call(s32[64]{0:T(128)} %select_reduce_fusion.inv, f32[1]{0:T(128)S(6)} %copy.8.lower, f32[1]{0:T(128)S(6)} %copy.9.upper, bf16[16,1024]{1,0:T(8,128)(2,1)} %start.1, bf16[64,128,128]{2,1,0:T(8,128)(2,1)} %bitcast.5, bf16[64,128,128]{2,1,0:T(8,128)(2,1)} %bitcast.6), custom_call_target="tpu_custom_call" | custom-call | tf_op jit(solution)/shard_map/filter/pallas_call | solution.py:181
  80.8 1.5 %copy.10 = f32[16,1024]{1,0:T(8,128)} copy(f32[16,1024]{1,0:T(8,128)} %filter.1) | data formatting | bytes 131072

commit v2 on v1

v2 whole, which is shorter than its diff:
```python
import jax
import jax.numpy as jnp
from jax import lax
from jax.experimental import pallas as pl
from jax.experimental.pallas import tpu as pltpu
from jax.sharding import PartitionSpec as P

MESH = pl.DeviceIdType.MESH
BLK = 128
BR = 8
TILE = 1024
PIECE = 16
G = 2
ROWS = PIECE // G
WIDE = TILE // G
ORDER = (
    (0, 0), (1, 0), (0, 1), (1, 1), (0, 2), (0, 3), (1, 2), (1, 3), (0, 4), (1, 4), (0, 5), (0, 6), (1, 5),
    (1, 6), (0, 7), (1, 7), (0, 8), (1, 8), (0, 9), (1, 9), (0, 10), (0, 11), (1, 10), (1, 11), (0, 12), (1, 12),
)
NS = 8
TOP = 32766.0
TINY = 1e-33
ROW_NEAR = (1, 7, 2, 6, 3, 5, 4)
ROW_FAR = (4, 3, 5, 2, 6, 1, 7)
COL_NEAR = (4, 1, 3, 5, 7, 2, 6)
COL_FAR = (6, 2, 5, 7, 1, 3, 4)


def back(axis, o):
    return (-o) % NS if axis == "row" else (o // 4) * 4 + (-o) % 4


def rem(a, b):
    return lax.rem(a, jnp.int32(b))


def div(a, b):
    return lax.div(a, jnp.int32(b))


def flip(bit, s):
    return 1 - bit if s else bit


def kernel(pairs, lower, upper, start_hbm, khbm, mhbm, out, first_out, start, place, limits, inv_wide, inv, kslot, mslot, kt, mt, kd, md, ybuf, ag, qsib, rsib, qring, rring, own, keep,
           s_sib, s_ring, r_sib, r_ring, local_sem, send_sem, recv_sem, ssend_sem, srecv_sem):
    r = lax.axis_index("row")
    c = lax.axis_index("col")
    xh, z = div(r, NS), rem(r, NS)
    y, xl, core = div(c, 4), rem(div(c, 2), 2), rem(c, 2)

    def member(axis, s, o):
        if axis == "row":
            return flip(xh, s) * NS + rem(z + o, NS)
        return rem(y + o % 4, 4) * 4 + flip(xl, o // 4) * 2 + flip(core, s)

    def device(axis, s, o):
        m = member(axis, s, o)
        return (m, c) if axis == "row" else (r, m)

    barrier = pltpu.get_barrier_semaphore()
    for axis in ("row", "col"):
        for o in range(1, NS):
            pl.semaphore_signal(barrier, inc=1, device_id=device(axis, 0, o), device_id_type=MESH)
        pl.semaphore_signal(barrier, inc=1, device_id=device(axis, 1, 0), device_id_type=MESH)

    loads = [
        pltpu.make_async_copy(src, dst, local_sem.at[i])
        for i, (src, dst) in enumerate(
            ((start_hbm, start), (pairs, place), (khbm, kslot), (mhbm, mslot),
             (lower, limits.at[0]), (upper, limits.at[1]))
        )
    ]
    for load in loads:
        load.start()

    def pack(part):
        return part if G == 1 else jnp.concatenate([part[:, :WIDE], part[:, WIDE:]], axis=0)

    def unpack(piece):
        return piece if G == 1 else jnp.concatenate([piece[:ROWS], piece[ROWS:]], axis=1)

    loads[0].wait()
    for g in range(G):
        keep[2, g] = pack(start[...].astype(jnp.float32)[g * ROWS:(g + 1) * ROWS]).astype(jnp.bfloat16)

    def build():
        slots = place.shape[1]
        target = lax.broadcasted_iota(jnp.int32, (BR * BR, slots), 0)
        slot = lax.broadcasted_iota(jnp.int32, (BR * BR, slots), 1)
        found = (place[0:1] == target // BR) & (place[1:2] == target % BR)
        held_by = jnp.max(jnp.where(found, slot, -1), axis=1, keepdims=True)
        inv_wide[...] = jnp.broadcast_to(held_by, inv_wide.shape)
        index = pltpu.make_async_copy(inv_wide, inv, local_sem.at[6])
        index.start()
        index.wait()
        loads[2].wait()
        loads[3].wait()
        for t in range(BR * BR):
            s = inv[t, 0]
            live = s >= 0
            s = jnp.maximum(s, 0)
            zero = jnp.zeros((BLK, BLK), jnp.bfloat16)
            rows, cols = slice((t // BR) * BLK, (t // BR + 1) * BLK), slice((t % BR) * BLK, (t % BR + 1) * BLK)
            kblock = jnp.where(live, kslot[s], zero)
            mblock = jnp.where(live, mslot[s], zero)
            kd[rows, cols] = kblock
            md[rows, cols] = mblock
            kt[cols, rows] = kblock.T
            mt[cols, rows] = mblock.T

    pl.semaphore_wait(barrier, 2 * NS)

    sent = []

    def copy(g, n, side, src, dst, i, j, dev, sems=(send_sem, recv_sem)):
        return pltpu.make_async_remote_copy(
            src_ref=src, dst_ref=dst, send_sem=sems[0].at[g, n, side, i], recv_sem=sems[1].at[g, n, side, j],
            device_id=dev, device_id_type=MESH)

    def push(*args, **kw):
        one = copy(*args, **kw)
        one.start()
        sent.append(one)

    def arrived(g, n, side, dst, j, sems=(send_sem, recv_sem)):
        copy(g, n, side, dst, dst, 0, j, (r, c), sems).wait_recv()

    def near(axis):
        return ROW_NEAR if axis == "row" else COL_NEAR

    def far(axis):
        return ROW_FAR if axis == "row" else COL_FAR

    def gather_send(g, m, n, axis, src):
        buf = ag.at[m, g]
        push(g, n, 1, src, buf.at[NS], 0, 0, device(axis, 1, 0))
        for o in ROW_NEAR if axis == "row" else COL_FAR:
            j = back(axis, o)
            push(g, n, 0, src, buf.at[j], o, j, device(axis, 0, o))
        buf[0] = src[...]

    def gather_pass(g, m, n, axis):
        buf = ag.at[m, g]
        for o in near(axis):
            arrived(g, n, 0, buf.at[o], o)
            push(g, n, 1, buf.at[o], buf.at[NS + o], o, o, device(axis, 1, 0))

    def gather_end(g, m, n, axis):
        for o in (0,) + near(axis):
            arrived(g, n, 1, ag.at[m, g, NS + o], o)

    def quantize(part, q, sc):
        top = jnp.maximum(jnp.max(jnp.abs(part), keepdims=True), TINY)
        q[...] = jnp.round(pack(part * (TOP / top))).astype(jnp.int32).astype(jnp.int16)
        sc[...] = jnp.broadcast_to(top * (1.0 / TOP), (1, BLK))

    def value(q, sc):
        return unpack(q[...].astype(jnp.int32).astype(jnp.float32)) * sc[:, :1]

    scale_sems = (ssend_sem, srecv_sem)

    def scatter_send(g, m, n, axis):
        for o in far(axis) + (0,):
            quantize(ybuf[g, NS + o], qsib.at[m, g, o], s_sib.at[m, g, o])
            push(g, n, 1, qsib.at[m, g, o], rsib.at[m, g, o], o, o, device(axis, 1, 0))
            push(g, n, 1, s_sib.at[m, g, o], r_sib.at[m, g, o], o, o, device(axis, 1, 0), scale_sems)

    def scatter_pass(g, m, n, axis):
        for o in far(axis) + (0,):
            arrived(g, n, 1, rsib.at[m, g, o], o)
            arrived(g, n, 1, r_sib.at[m, g, o], o, scale_sems)
            part = ybuf[g, o] + value(rsib.at[m, g, o], r_sib.at[m, g, o])
            if o:
                j = back(axis, o)
                quantize(part, qring.at[m, g, o], s_ring.at[m, g, o])
                push(g, n, 0, qring.at[m, g, o], rring.at[m, g, j], o, j, device(axis, 0, o))
                push(g, n, 0, s_ring.at[m, g, o], r_ring.at[m, g, j], o, j, device(axis, 0, o), scale_sems)
            else:
                own[g] = part

    def scatter_end(g, m, n, axis):
        total = own[g]
        for o in near(axis):
            arrived(g, n, 0, rring.at[m, g, o], o)
            arrived(g, n, 0, r_ring.at[m, g, o], o, scale_sems)
            total = total + value(rring.at[m, g, o], r_ring.at[m, g, o])
        return total

    def product(g, m, come, go, scale, transposed):
        low, high = limits[0], limits[1]
        centre, half = 0.5 * (low + high), 0.5 * (high - low)
        rows = []
        for s in (0, 1):
            for o in range(NS):
                v = member(go, s, o)
                if come == "row":
                    slot = rem(div(v, NS) + xh, 2) * NS + rem(rem(v, NS) - z + NS, NS)
                else:
                    slot = rem(v + core, 2) * NS + rem(div(v, 2) + xl, 2) * 4 + rem(div(v, 4) - y + 4, 4)
                rows.append(unpack(ag[m, g, slot].astype(jnp.float32)) if G > 1 else ag[m, g, slot])
        x = jnp.concatenate(rows, axis=0).astype(jnp.bfloat16)
        kpart = jnp.dot(x, (kt if transposed else kd)[...], preferred_element_type=jnp.float32)
        mpart = jnp.dot(x, (mt if transposed else md)[...], preferred_element_type=jnp.float32)
        ybuf[g] = ((kpart - centre * mpart) * (scale / half)).reshape(2 * NS, ROWS, TILE)

    def held(m, g):
        return unpack(keep[m, g].astype(jnp.float32))

    def step(g, t):
        rows = slice(g * ROWS, (g + 1) * ROWS)
        if t == 0:
            gather_send(g, 0, 0, "row", keep.at[2, g])
        elif t == 1:
            gather_pass(g, 0, 0, "row")
        elif t == 2:
            gather_end(g, 0, 0, "row")
            product(g, 0, "row", "col", 1.0, True)
            scatter_send(g, 0, 1, "col")
        elif t == 3:
            scatter_pass(g, 0, 1, "col")
        elif t == 4:
            keep[0, g] = pack(scatter_end(g, 0, 1, "col")).astype(jnp.bfloat16)
            gather_send(g, 1, 2, "col", keep.at[0, g])
        elif t == 5:
            gather_pass(g, 1, 2, "col")
        elif t == 6:
            gather_end(g, 1, 2, "col")
            product(g, 1, "col", "row", 2.0, False)
            scatter_send(g, 1, 3, "row")
        elif t == 7:
            scatter_pass(g, 1, 3, "row")
        elif t == 8:
            keep[1, g] = pack(scatter_end(g, 1, 3, "row") - held(2, g)).astype(jnp.bfloat16)
            gather_send(g, 2, 4, "row", keep.at[1, g])
        elif t == 9:
            gather_pass(g, 2, 4, "row")
        elif t == 10:
            gather_end(g, 2, 4, "row")
            product(g, 2, "row", "col", 2.0, True)
            scatter_send(g, 2, 5, "col")
        elif t == 11:
            scatter_pass(g, 2, 5, "col")
        else:
            out[rows] = scatter_end(g, 2, 5, "col")
            first_out[rows] = held(0, g)

    for n, (g, t) in enumerate(ORDER):
        if n == G:
            for load in (loads[1], loads[4], loads[5]):
                load.wait()
            build()
        step(g, t)
    for one in sent:
        one.wait_send()


def local(start, stiffness, mass, coords, lower, upper):
    slots = stiffness.shape[2]
    vmem, hbm = (pl.BlockSpec(memory_space=m) for m in (pltpu.VMEM, pl.ANY))
    half = (3, G, NS, PIECE, WIDE)
    scales = pltpu.VMEM((3, G, NS, 1, BLK), jnp.float32)
    sems = pltpu.SemaphoreType.DMA((G, 6, 2, NS))
    total, first = pl.pallas_call(
        kernel,
        out_shape=[jax.ShapeDtypeStruct(start.shape, jnp.float32)] * 2,
        in_specs=[hbm] * 6,
        out_specs=[vmem] * 2,
        scratch_shapes=[
            pltpu.VMEM(start.shape, start.dtype),
            pltpu.VMEM((2, slots), jnp.int32),
            pltpu.VMEM((2, 1, 1), jnp.float32),
            pltpu.VMEM((BR * BR, BLK), jnp.int32),
            pltpu.SMEM((BR * BR, BLK), jnp.int32),
            pltpu.VMEM((slots, BLK, BLK), jnp.bfloat16),
            pltpu.VMEM((slots, BLK, BLK), jnp.bfloat16),
            pltpu.VMEM((TILE, TILE), jnp.bfloat16),
            pltpu.VMEM((TILE, TILE), jnp.bfloat16),
            pltpu.VMEM((TILE, TILE), jnp.bfloat16),
            pltpu.VMEM((TILE, TILE), jnp.bfloat16),
            pltpu.VMEM((G, 2 * NS, ROWS, TILE), jnp.float32),
            pltpu.VMEM((3, G, 2 * NS, PIECE, WIDE), jnp.bfloat16),
            pltpu.VMEM(half, jnp.int16),
            pltpu.VMEM(half, jnp.int16),
            pltpu.VMEM(half, jnp.int16),
            pltpu.VMEM(half, jnp.int16),
            pltpu.VMEM((G, ROWS, TILE), jnp.float32),
            pltpu.VMEM((3, G, PIECE, WIDE), jnp.bfloat16),
            scales, scales, scales, scales,
            pltpu.SemaphoreType.DMA((7,)),
            sems, sems, sems, sems,
        ],
        compiler_params=pltpu.CompilerParams(
            collective_id=0, has_side_effects=True, vmem_limit_bytes=56 * 2**20
        ),
        name="filter",
    )(coords[0, 0].T, lower.reshape(1, 1), upper.reshape(1, 1), start,
      stiffness.reshape(stiffness.shape[2:]), mass.reshape(mass.shape[2:]))
    return total - first


def solution(mesh):
    placed = (
        P("row", "col"),
        P("row", "col", None, None, None),
        P("row", "col", None, None, None),
        P("row", "col", None, None),
        P(),
        P(),
    )
    return jax.shard_map(
        local, mesh=mesh, in_specs=placed, out_specs=P("col", "row"), check_vma=False
    )
```

time: 82.5 us -> 74.1 us (0.90)
  Pallas kernels: 78.1 us -> 71.1 us
  local copies, waits for them, and re-layouts: 1.47 us -> 0 us
    pallas_call x1, Pallas kernels: 78.1 us -> 71.1 us  [local(): pl.pallas_call(kernel, out_shape=[jax.ShapeDtypeStruct(start.shape, jnp.f...]
    sub x0 -> x1, other arithmetic: none -> 1.51 us  [local(): return total - first]
    unnamed x1 -> x0, local copies, waits for them, and re-layouts: 1.47 us -> none
where the time goes in v2:
time: 74.1 us; the launch traced here: 74 us
  Pallas kernels  71.1 us (96%)
  other arithmetic  1.51 us (2%)
  between operations  1.3 us (2%)
    pallas_call x1, Pallas kernels, local(): pl.pallas_call(kernel, out_shape=[jax.ShapeDtypeStruct(start.shape, jnp.f...  71.1 us
    sub x1, other arithmetic, local(): return total - first  1.51 us

profile of v2, /device:TPU:1, one launch (start us, length us, event | category | flops | bytes accessed | tf_op | source)
XLA Modules:
  0.0 74.0 jit_solution(13123720556499280457)
XLA Ops:
  1.3 71.1 %filter.1 = (f32[16,1024]{1,0:T(8,128)}, f32[16,1024]{1,0:T(8,128)}) custom-call(s32[2,64]{1,0:T(2,128)} %bitcast.11, f32[1,1]{1,0:T(1,128)} %bitcast.7.lower, f32[1,1]{1,0:T(1,128)} %bitcast.8.upper, bf16[16,1024]{1,0:T(8,128)(2,1)} %start_hbm.1, bf16[64,128,128]{2,1,0:T(8,128)(2,1)} %bitcast.9, bf16[64,128,128]{2,1,0:T(8,128)(2,1)} %bitcast.10), custom_call_target="tpu_custom_call" | custom-call | tf_op jit(solution)/shard_map/filter/pallas_call | solution.py:264
  72.4 1.5 %sub.3 = f32[16,1024]{1,0:T(8,128)} subtract(f32[16,1024]{1,0:T(8,128)} %get-tuple-element.7, f32[16,1024]{1,0:T(8,128)} %get-tuple-element.8) | non-fusion elementwise | flops 16384 | bytes 196608 | tf_op jit(solution)/shard_map/sub | solution.py:299

commit v3 on v2

--- a/solution.py
+++ b/solution.py
@@ -246,7 +246,7 @@
             first_out[rows] = held(0, g)
 
     for n, (g, t) in enumerate(ORDER):
-        if n == G:
+        if n == 1:
             for load in (loads[1], loads[4], loads[5]):
                 load.wait()
             build()
@@ -263,7 +263,7 @@
     sems = pltpu.SemaphoreType.DMA((G, 6, 2, NS))
     total, first = pl.pallas_call(
         kernel,
-        out_shape=[jax.ShapeDtypeStruct(start.shape, jnp.float32)] * 2,
+        out_shape=[pltpu.VMEM(start.shape, jnp.float32)] * 2,
         in_specs=[hbm] * 6,
         out_specs=[vmem] * 2,
         scratch_shapes=[
@@ -291,7 +291,7 @@
             sems, sems, sems, sems,
         ],
         compiler_params=pltpu.CompilerParams(
-            collective_id=0, has_side_effects=True, vmem_limit_bytes=56 * 2**20
+            collective_id=0, has_side_effects=True, vmem_limit_bytes=57344 * 2**10
         ),
         name="filter",
     )(coords[0, 0].T, lower.reshape(1, 1), upper.reshape(1, 1), start,

time: 74.1 us -> 71.9 us (0.970)
  Pallas kernels: 71.1 us -> 69.9 us
  other arithmetic: 1.51 us -> 0.64 us
    pallas_call x1, Pallas kernels: 71.1 us -> 69.9 us  [local(): pl.pallas_call(kernel, out_shape=[pltpu.VMEM(start.shape, jnp.float32)] *...]
    sub x1, other arithmetic: 1.51 us -> 0.64 us  [local(): return total - first]
where the time goes in v3:
time: 71.9 us; the launch traced here: 71.8 us
  Pallas kernels  69.9 us (97%)
  between operations  1.3 us (2%)
    pallas_call x1, Pallas kernels, local(): pl.pallas_call(kernel, out_shape=[pltpu.VMEM(start.shape, jnp.float32)] *...  69.9 us

profile of v3, /device:TPU:1, one launch (start us, length us, event | category | flops | bytes accessed | tf_op | source)
XLA Modules:
  0.0 71.8 jit_solution(13493686545315066507)
XLA Ops:
  1.3 69.9 %filter.1 = (f32[16,1024]{1,0:T(8,128)S(1)}, f32[16,1024]{1,0:T(8,128)S(1)}) custom-call(s32[2,64]{1,0:T(2,128)} %bitcast.11, f32[1,1]{1,0:T(1,128)} %bitcast.7.lower, f32[1,1]{1,0:T(1,128)} %bitcast.8.upper, bf16[16,1024]{1,0:T(8,128)(2,1)} %start_hbm.1, bf16[64,128,128]{2,1,0:T(8,128)(2,1)} %bitcast.9, bf16[64,128,128]{2,1,0:T(8,128)(2,1)} %bitcast.10), custom_call_target="tpu_custom_call" | custom-call | tf_op jit(solution)/shard_map/filter/pallas_call | solution.py:264
  71.2 0.6 sub.3

commit v4 on v3

--- a/solution.py
+++ b/solution.py
@@ -18,6 +18,7 @@
     (1, 6), (0, 7), (1, 7), (0, 8), (1, 8), (0, 9), (1, 9), (0, 10), (0, 11), (1, 10), (1, 11), (0, 12), (1, 12),
 )
 NS = 8
+LATE = 5
 TOP = 32766.0
 TINY = 1e-33
 ROW_NEAR = (1, 7, 2, 6, 3, 5, 4)
@@ -245,13 +246,18 @@
             out[rows] = scatter_end(g, 2, 5, "col")
             first_out[rows] = held(0, g)
 
+    marks = []
     for n, (g, t) in enumerate(ORDER):
         if n == 1:
             for load in (loads[1], loads[4], loads[5]):
                 load.wait()
             build()
         step(g, t)
-    for one in sent:
+        marks.append(len(sent))
+        if n >= LATE:
+            for one in sent[marks[n - LATE - 1] if n > LATE else 0:marks[n - LATE]]:
+                one.wait_send()
+    for one in sent[marks[len(ORDER) - 1 - LATE]:]:
         one.wait_send()
 
 

time: 71.9 us -> 71.2 us (level)
  no operation moved by 1% of the time
where the time goes in v4:
time: 71.2 us; the launch traced here: 71.1 us
  Pallas kernels  69.2 us (97%)
  between operations  1.3 us (2%)
    pallas_call x1, Pallas kernels, local(): pl.pallas_call(kernel, out_shape=[pltpu.VMEM(start.shape, jnp.float32)] *...  69.2 us

profile of v4, /device:TPU:1, one launch (start us, length us, event | category | flops | bytes accessed | tf_op | source)
XLA Modules:
  0.0 71.1 jit_solution(15361056490252619731)
XLA Ops:
  1.3 69.2 %filter.1 = (f32[16,1024]{1,0:T(8,128)S(1)}, f32[16,1024]{1,0:T(8,128)S(1)}) custom-call(s32[2,64]{1,0:T(2,128)} %bitcast.11, f32[1,1]{1,0:T(1,128)} %bitcast.7.lower, f32[1,1]{1,0:T(1,128)} %bitcast.8.upper, bf16[16,1024]{1,0:T(8,128)(2,1)} %start_hbm.1, bf16[64,128,128]{2,1,0:T(8,128)(2,1)} %bitcast.9, bf16[64,128,128]{2,1,0:T(8,128)(2,1)} %bitcast.10), custom_call_target="tpu_custom_call" | custom-call | tf_op jit(solution)/shard_map/filter/pallas_call | solution.py:270
  70.5 0.6 sub.3
